TPU v7x, 32 devices: a whole 2x2x4 slice. The times are simulated.
32 devices in a mesh: dp: 2 (over x), seq: 16 (over z, y, core).
Axes of the slice: x: 2, y: 2, z: 4, core: 2. Of those that a mesh axis runs over, the one named last changes fastest.
Arguments:
- tokens: bfloat16 [6144, 4096], P(('dp', 'seq')), parts along dimension 0, may hold values from -72 to 72
- monarch_inner_factor: bfloat16 [3, 64, 64, 64], replicated, may hold values from -0.75 to 0.75
- monarch_outer_factor: bfloat16 [3, 64, 64, 64], replicated, may hold values from -0.75 to 0.75
- adapter_down_weight: bfloat16 [3, 4096, 16], replicated, may hold values from -0.09375 to 0.09375
- adapter_up_weight: bfloat16 [3, 16, 4096], replicated, may hold values from -1.5 to 1.5
- pattern: int32 [96, 3], P('dp'), parts along dimension 0, may hold values from 2 to 47, as said below
Outputs:
- context: bfloat16 [6144, 4096], P(('dp', 'seq')), parts along dimension 0
There are 2 independent parts, one for each index of `dp`. A program takes and returns all parts, laid end to end along the dimension named above; an argument that names none is the same for every part. Nothing has to cross between parts.
Inputs may be any that keep to these rules, and one draw needn't show every extreme that they name: `pattern`: row b names the random key blocks of query block b. The 9 entries of the rows of one index of seq name at most 1 block held by any one index of seq, and exactly 1 of some index's blocks. A block may be named more than once.
All inputs are finite; a program needn't handle non-finite values.
Results may differ from a plain program's by a relative error of at most 0.012.
The roundings to bfloat16 on the way count: a program that leaves them out, or rounds other values in their place, can miss the bound.
Values may be sent and summed in bfloat16 or wider, within the bound.
A program may use at most 192 MiB of HBM per device.

v0:
```python
import jax
import jax.numpy as jnp
from jax import lax
from jax.sharding import PartitionSpec as P

HEADS = 32
HD = 128
BLK = 64
RAND = 3
GLOB_BLOCKS = 2


def spread(value, axis, root):
    mine = lax.axis_index(axis) == root
    return lax.psum(jnp.where(mine, value, jnp.zeros_like(value)), axis)


def padded_2(value, sides, width):
    for axis, dim in sides:
        size, length = (lax.axis_size(axis), value.shape[dim])
        up = [(i, (i + 1) % size) for i in range(size - 1)]
        down = [(j, i) for i, j in up]
        last = lax.slice_in_dim(value, length - width, length, axis=dim)
        initial = lax.slice_in_dim(value, 0, width, axis=dim)
        before = lax.ppermute(last, axis, up)
        after = lax.ppermute(initial, axis, down)
        value = jnp.concatenate([before, value, after], axis=dim)
    return value


def combined_all(value, axis, join):
    pieces = jax.tree.map(lambda part: lax.all_gather(part, axis), value)
    head = jax.tree.map(lambda part: part[0], pieces)
    tail = jax.tree.map(lambda part: part[1:], pieces)
    so_far, _ = lax.scan(lambda so_far, piece: (join(so_far, piece), None), head, tail)
    return so_far


def apply_projection(
    tokens, monarch_inner_factor, monarch_outer_factor, adapter_down_weight, adapter_up_weight
):
    row_count, feature_count = tokens.shape
    proj_count = monarch_inner_factor.shape[0]
    block_count = monarch_inner_factor.shape[1]
    split_rows = tokens.reshape(row_count, block_count, block_count)
    inner_rows = jnp.einsum(
        "tai,paij->ptaj", split_rows, monarch_inner_factor, preferred_element_type=jnp.float32
    ).astype(jnp.bfloat16)
    main_part = jnp.einsum(
        "ptaj,pjak->ptjk", inner_rows, monarch_outer_factor, preferred_element_type=jnp.float32
    )
    adapter_update = jnp.einsum(
        "kg,vgj->vkj", tokens, adapter_down_weight, preferred_element_type=jnp.float32
    ).astype(jnp.bfloat16)
    adapter_lifted_rows = jnp.einsum(
        "bcj,bjf->bcf", adapter_update, adapter_up_weight, preferred_element_type=jnp.float32
    )
    return (main_part.reshape(proj_count, row_count, feature_count) + adapter_lifted_rows).astype(
        jnp.bfloat16
    )


def to_heads(rows):
    proj_count, row_count, feature_count = rows.shape
    return jnp.transpose(
        rows.reshape(proj_count, row_count, HEADS, feature_count // HEADS), (0, 2, 1, 3)
    )


def combine(part_one, part_two):
    peak_one, total_one, numer_one = part_one
    peak_two, total_two, numer_two = part_two
    joint_peak = jnp.maximum(peak_one, peak_two)
    factor_one = jnp.exp(peak_one - joint_peak)
    factor_two = jnp.exp(peak_two - joint_peak)
    joint_total = total_one * factor_one + total_two * factor_two
    joint_numer = numer_one * factor_one[:, :, None] + numer_two * factor_two[:, :, None]
    return (joint_peak, joint_total, joint_numer)


def per_device(
    tokens,
    monarch_inner_factor,
    monarch_outer_factor,
    adapter_down_weight,
    adapter_up_weight,
    pattern,
):
    tok_rows, feature_count = tokens.shape
    head_size = feature_count // HEADS
    local_blocks = tok_rows // BLK
    seq_count = lax.axis_size("seq")
    seq_index = lax.axis_index("seq")
    block_total = seq_count * local_blocks
    global_rows = GLOB_BLOCKS * BLK
    request_count = local_blocks * RAND
    slot_count = (request_count + seq_count - 1) // seq_count
    score_scale = float(HD) ** (-0.5)
    kv_right = monarch_inner_factor[1:]
    kv_left = monarch_outer_factor[1:]
    kv_down = adapter_down_weight[1:]
    kv_up = adapter_up_weight[1:]
    projected_rows = apply_projection(
        tokens, monarch_inner_factor, monarch_outer_factor, adapter_down_weight, adapter_up_weight
    )
    head_rows_all = to_heads(projected_rows)
    key_value = head_rows_all[1:]
    picked = pattern.reshape(seq_count, request_count)
    source_dev = picked // local_blocks
    within = picked % local_blocks
    req_order = jnp.arange(request_count, dtype=jnp.int32)
    same_source = source_dev[:, :, None] == source_dev[:, None, :]
    earlier = req_order[None, :] < req_order[:, None]
    slot_rank = jnp.sum((same_source & earlier[None]).astype(jnp.int32), axis=2)
    slot_ids = jnp.arange(slot_count, dtype=jnp.int32)
    matches = (source_dev == seq_index)[:, None, :] & (
        slot_rank[:, None, :] == slot_ids[None, :, None]
    )
    present = jnp.any(matches, axis=2)
    chosen = jnp.sum(jnp.where(matches, within[:, None, :], 0), axis=2)
    my_source = lax.dynamic_index_in_dim(source_dev, seq_index, 0, keepdims=False)
    my_rank = lax.dynamic_index_in_dim(slot_rank, seq_index, 0, keepdims=False)
    fetch_index = my_source * slot_count + my_rank
    zero_value = jnp.zeros((), jnp.bfloat16)
    global_tokens = spread(tokens[:global_rows], "seq", 0)
    global_heads = to_heads(
        apply_projection(
            global_tokens,
            monarch_inner_factor,
            monarch_outer_factor,
            adapter_down_weight,
            adapter_up_weight,
        )
    )
    padded_tokens = padded_2(tokens, (("seq", 0),), BLK)
    rim_tokens = jnp.concatenate([padded_tokens[:BLK], padded_tokens[BLK + tok_rows :]], axis=0)
    rim_kv = to_heads(apply_projection(rim_tokens, kv_right, kv_left, kv_down, kv_up))
    padded = jnp.concatenate([rim_kv[:, :, :BLK], key_value, rim_kv[:, :, BLK:]], axis=2)
    token_blocks = tokens.reshape(local_blocks, BLK, feature_count)
    outgoing = jnp.take(token_blocks, chosen.reshape(-1), axis=0).reshape(
        seq_count, slot_count, BLK, feature_count
    )
    outgoing = jnp.where(present[:, :, None, None], outgoing, zero_value)
    incoming = lax.all_to_all(outgoing, "seq", split_axis=0, concat_axis=0, tiled=True)
    fetched = jnp.take(
        incoming.reshape(seq_count * slot_count, BLK, feature_count), fetch_index, axis=0
    )
    random_flat = apply_projection(
        fetched.reshape(request_count * BLK, feature_count), kv_right, kv_left, kv_down, kv_up
    )
    random_kv = to_heads(random_flat)
    random_keys = random_kv.reshape(2, HEADS, local_blocks, RAND * BLK, head_size)
    padded_blocks = padded.reshape(2, HEADS, local_blocks + 2, BLK, head_size)
    local_kv = jnp.concatenate(
        [
            padded_blocks[:, :, 0:local_blocks],
            padded_blocks[:, :, 1 : local_blocks + 1],
            padded_blocks[:, :, 2 : local_blocks + 2],
            random_keys,
        ],
        axis=3,
    )
    block_ids = seq_index * local_blocks + jnp.arange(local_blocks, dtype=jnp.int32)
    window_blocks = block_ids[:, None] + jnp.arange(-1, 2, dtype=jnp.int32)[None, :]
    window_valid = (window_blocks >= GLOB_BLOCKS) & (window_blocks < block_total)
    always_random = jnp.zeros((local_blocks, RAND * BLK), jnp.int32) == 0
    key_valid = jnp.concatenate([jnp.repeat(window_valid, BLK, axis=1), always_random], axis=1)
    query_blocks = head_rows_all[0].reshape(HEADS, local_blocks, BLK, head_size)
    global_keys = global_heads[1]
    global_values = global_heads[2]
    local_scores = (
        jnp.einsum("hbqe,hbke->hbqk", query_blocks, local_kv[0], preferred_element_type=jnp.float32)
        * score_scale
    )
    local_scores = jnp.where(key_valid[None, :, None, :], local_scores, -jnp.inf)
    glob_scores = (
        jnp.einsum("hbqe,hge->hbqg", query_blocks, global_keys, preferred_element_type=jnp.float32)
        * score_scale
    )
    row_peak = jnp.maximum(jnp.max(local_scores, axis=-1), jnp.max(glob_scores, axis=-1))
    local_weights = jnp.exp(local_scores - row_peak[..., None])
    glob_weights = jnp.exp(glob_scores - row_peak[..., None])
    row_total = jnp.sum(local_weights, axis=-1) + jnp.sum(glob_weights, axis=-1)
    local_numer = jnp.einsum(
        "hbqk,hbke->hbqe",
        local_weights.astype(jnp.bfloat16),
        local_kv[1],
        preferred_element_type=jnp.float32,
    )
    glob_numer = jnp.einsum(
        "hbqg,hge->hbqe",
        glob_weights.astype(jnp.bfloat16),
        global_values,
        preferred_element_type=jnp.float32,
    )
    mixed = (local_numer + glob_numer) / row_total[..., None]
    local_out = (
        jnp.transpose(mixed.reshape(HEADS, tok_rows, head_size), (1, 0, 2))
        .reshape(tok_rows, feature_count)
        .astype(jnp.bfloat16)
    )
    global_query = global_heads[0]
    global_scores = (
        jnp.einsum(
            "hqe,hke->hqk", global_query, head_rows_all[1], preferred_element_type=jnp.float32
        )
        * score_scale
    )
    global_peak = jnp.max(global_scores, axis=-1)
    global_weights = jnp.exp(global_scores - global_peak[:, :, None])
    global_total = jnp.sum(global_weights, axis=-1)
    global_numer = jnp.einsum(
        "hqk,hke->hqe",
        global_weights.astype(jnp.bfloat16),
        head_rows_all[2],
        preferred_element_type=jnp.float32,
    )
    merged = combined_all((global_peak, global_total, global_numer), "seq", combine)
    head_mixed = merged[2] / merged[1][:, :, None]
    head_out = (
        jnp.transpose(head_mixed, (1, 0, 2))
        .reshape(global_rows, feature_count)
        .astype(jnp.bfloat16)
    )
    head_rows = jnp.where(seq_index == 0, head_out, local_out[:global_rows])
    return jnp.concatenate([head_rows, local_out[global_rows:]], axis=0)


def solution(mesh):
    return jax.shard_map(
        per_device,
        mesh=mesh,
        in_specs=(P(("dp", "seq"), None), P(), P(), P(), P(), P("dp", None)),
        out_specs=P(("dp", "seq"), None),
        check_vma=False,
    )
```

profile of v0, /device:TPU:1, one launch (start us, length us, event | category | flops | bytes accessed | tf_op | source)
XLA Modules:
  0.0 794.4 jit_solution(10107030205447234315)
XLA Ops:
  11.5 7.1 convert_bitcast_fusion.1
  18.6 12.5 %fusion.15 = f32[3,64,192,64]{2,3,1,0:T(8,128)} fusion(bf16[3,64,64,64]{3,2,1,0:T(8,128)(2,1)S(1)} %copy-done.1, bf16[3,192,64,64]{1,3,0,2:T(8,128)(2,1)} %convert_bitcast_fusion.1), kind=kOutput, calls=%fused_computation.31 | convolution fusion | flops 301989888 | bytes 15728640 | tf_op jit(solution)/shard_map/ptaj,pjak->ptjk/dot_general | solution.py:49
  31.1 11.7 %copy.123 = f32[3,192,4096]{2,1,0:T(8,128)} copy(f32[3,192,4096]{1,2,0:T(8,128)} %bitcast.205) | data formatting | bytes 18874368 | tf_op jit(solution)/shard_map/reshape | solution.py:58
  42.9 8.1 %fusion.34 = bf16[3,24,32,8,128]{4,3,2,1,0:T(8,128)(2,1)} fusion(f32[3,192,4096]{2,1,0:T(8,128)} %copy.123, bf16[3,16,4096]{2,1,0:T(8,128)(2,1)S(1)} %copy-done.13, bf16[3,4096,16]{1,2,0:T(8,128)(2,1)S(1)} %copy-done.15, bf16[192,4096]{1,0:T(8,128)(2,1)S(1)} %copy-done), kind=kOutput, calls=%fused_computation.60 | convolution fusion | flops 155722752 | bytes 16515072 | tf_op jit(solution)/shard_map/bcj,bjf->bcf/dot_general | solution.py:55
  51.0 5.9 copy.197
  56.9 48.8 %all-reduce.3.cloned.1.call-done = bf16[128,4096]{1,0:T(8,128)(2,1)} async-done(((bf16[128,4096]{1,0:T(8,128)(2,1)}), bf16[128,4096]{1,0:T(8,128)(2,1)}) %all-reduce.3.cloned.1.call-update) | async-done | bytes 1048592 | tf_op jit(solution)/shard_map/psum | solution.py:15
  110.5 6.1 fusion.23
  116.7 6.6 copy.117
  137.1 4.7 gather_fusion
  141.7 8.7 %fusion.9 = bf16[16,1,64,4096]{3,2,1,0:T(8,128)(2,1)} fusion(bf16[16,64,4096]{2,1,0:T(8,128)(2,1)} %gather_fusion, pred[16]{0:T(512)(128)(4,1)S(1)} %compare_and_fusion, pred[16]{0:T(512)(128)(4,1)S(1)} %get-tuple-element.63), kind=kLoop, calls=%fused_computation.27 | loop fusion | flops 8388608 | bytes 16777248 | tf_op jit(solution)/shard_map/jit(_where)/select_n | solution.py:143
  150.4 5.4 all-to-all-start
  184.9 254.3 %all-gather = f32[512,128]{1,0:T(8,128)S(1)} all-gather(f32[32,128]{1,0:T(8,128)S(1)} %get-tuple-element.80), channel_id=2, replica_groups=mesh['dp'=2,'seq'=16] {'seq'}, dimensions={0}, use_global_device_ids=true | all-gather | bytes 278528 | tf_op jit(solution)/shard_map/all_gather | solution.py:32
  441.1 35.9 %all-gather.1 = f32[512,128]{1,0:T(8,128)S(1)} all-gather(f32[32,128]{1,0:T(8,128)S(1)} %fusion.29), channel_id=3, replica_groups=mesh['dp'=2,'seq'=16] {'seq'}, dimensions={0}, use_global_device_ids=true | all-gather | bytes 278528 | tf_op jit(solution)/shard_map/all_gather | solution.py:32
  485.0 4.3 fusion.35
  489.4 5.7 copy.129
  513.3 4.4 multiply_reduce_fusion
  521.7 7.2 gather_fusion.1
  528.9 13.8 %gather.17 = bf16[576,64,64]{2,1,0:T(8,128)(2,1)} reshape(bf16[9,64,4096]{2,1,0:T(8,128)(2,1)} %gather_fusion.1) | data formatting | bytes 9437184 | tf_op jit(solution)/shard_map/jit(_take)/gather | solution.py:145
  542.7 5.9 select_bitcast_fusion
  548.6 25.0 %convert_bitcast_fusion = bf16[2,576,64,64]{1,3,0,2:T(8,128)(2,1)} fusion(bf16[2,64,64,64]{2,3,0,1:T(8,128)(2,1)} %copy.169, bf16[576,64,64,1]{2,1,0,3:T(8,128)(2,1)S(1)} %select_bitcast_fusion), kind=kOutput, calls=%fused_computation.14 | convolution fusion | flops 608698368 | bytes 15204352 | tf_op jit(solution)/shard_map/tai,paij->ptaj/dot_general | solution.py:46
  573.6 23.8 %fusion.3 = f32[2,64,576,64]{2,3,1,0:T(8,128)} fusion(bf16[2,576,64,64]{1,3,0,2:T(8,128)(2,1)} %convert_bitcast_fusion, bf16[3,64,64,64]{3,2,1,0:T(8,128)(2,1)S(1)} %copy-done.3), kind=kOutput, calls=%fused_computation.12 | convolution fusion | flops 603979776 | bytes 30408704 | tf_op jit(solution)/shard_map/ptaj,pjak->ptjk/dot_general | solution.py:49
  597.5 19.3 %copy.150 = f32[2,576,4096]{2,1,0:T(8,128)} copy(f32[2,576,4096]{1,2,0:T(8,128)} %bitcast.204) | data formatting | bytes 37748736 | tf_op jit(solution)/shard_map/reshape | solution.py:58
  621.1 10.6 %add_convert_fusion = bf16[2,576,4096]{2,1,0:T(8,128)(2,1)} fusion(f32[2,576,4096]{2,1,0:T(8,128)} %copy.150, bf16[3,16,4096]{2,1,0:T(8,128)(2,1)S(1)} %copy-done.13, f32[576,2,16]{0,2,1:T(8,128)S(1)} %bitcast.236), kind=kOutput, calls=%fused_computation.11 | convolution fusion | flops 160450560 | bytes 28655616 | tf_op jit(solution)/shard_map/bcj,bjf->bcf/dot_general | solution.py:55
  631.6 10.5 %copy.174 = bf16[144,8,32,128]{3,2,1,0:T(8,128)(2,1)} copy(bf16[144,8,32,128]{3,1,2,0:T(8,128)(2,1)} %bitcast.208) | data formatting | bytes 18874368
  642.1 8.9 %bitcast_bitcast_fusion = bf16[2,32,576,128]{3,1,2,0:T(8,128)(2,1)} fusion(bf16[2,576,32,128]{3,2,1,0:T(8,128)(2,1)} %bitcast.209), kind=kLoop, calls=%fused_computation.15 | loop fusion | bytes 18874368 | tf_op jit(solution)/shard_map/transpose | solution.py:65
  651.0 10.9 %copy.151 = bf16[2,32,576,128]{3,2,1,0:T(8,128)(2,1)} copy(bf16[2,32,576,128]{3,1,2,0:T(8,128)(2,1)} %bitcast_bitcast_fusion) | data formatting | bytes 18874368 | tf_op jit(solution)/shard_map/transpose | solution.py:65
  661.9 16.7 %pad_maximum_fusion = bf16[2,32,3,384,128]{4,3,2,1,0:T(8,128)(2,1)} fusion(bf16[2,32,3,192,128]{4,3,2,1,0:T(8,128)(2,1)} %bitcast.210, bf16[2,32,3,64,128]{4,3,2,1,0:T(8,128)(2,1)} %get-tuple-element.68, bf16[2,32,3,64,128]{4,3,2,1,0:T(8,128)(2,1)} %get-tuple-element.69, bf16[2,32,3,64,128]{4,3,2,1,0:T(8,128)(2,1)} %get-tuple-element.67), kind=kLoop, calls=%fused_computation.10 | loop fusion | flops 75497472 | bytes 37748736 | tf_op jit(solution)/shard_map/concatenate | solution.py:154
  678.6 7.3 fusion.10
  686.0 5.2 fusion.30
  694.0 10.5 %fusion.5 = f32[32,3,64,128]{3,2,1,0:T(8,128)} fusion(bf16[2,32,3,384,128]{4,3,2,1,0:T(8,128)(2,1)} %pad_maximum_fusion, f32[32,3,64,384]{3,2,1,0:T(8,128)} %copy-done.4, f32[32,3,64]{2,1,0:T(4,128)S(1)} %max.10, pred[3,384]{1,0:T(4,128)(4,1)S(1)} %copy-done.21), kind=kOutput, calls=%fused_computation.17 | convolution fusion | flops 613416960 | bytes 22045824 | tf_op jit(solution)/shard_map/hbqk,hbke->hbqe/dot_general | solution.py:184
  709.2 22.7 %slice.139 = f32[480,128,128]{2,1,0:T(8,128)} slice(f32[512,128,128]{2,1,0:T(8,128)} %all-gather.5.cloned.1.call-done), slice={[32:512], [0:128], [0:128]} | slice | bytes 62914560 | tf_op jit(solution)/shard_map/slice | solution.py:34
  731.9 52.2 %while.14 = (s32[]{:T(128)}, f32[32,128]{1,0:T(8,128)S(1)}, f32[32,128]{1,0:T(8,128)S(1)}, f32[32,128,128]{2,1,0:T(8,128)S(1)}, f32[15,32,128]{2,1,0:T(8,128)}, ...) while((s32[]{:T(128)}, f32[32,128]{1,0:T(8,128)S(1)}, f32[32,128]{1,0:T(8,128)S(1)}, ...), condition=%wide.region_4.5_spmd, body=%wide.region_3.4_spmd.sunk | while | flops 1597442 | bytes 6455397 | solution.py:35
  (173 shorter events, 151.1 us)
Async XLA Ops:
  6.5 2.5 copy-start
  6.5 99.1 %all-reduce.3.cloned.1.call-start = ((), (), s32[]{:S(2)}) async-start(), calls=%async_computation.1 | async-start | bytes 2097152 | tf_op jit(solution)/shard_map/psum | solution.py:15
  8.9 700.2 %all-gather.5.cloned.1.call-start = ((), (), s32[]{:S(2)}) async-start(), calls=%async_computation.2 | async-start | bytes 35651584 | tf_op jit(solution)/shard_map/all_gather | solution.py:32
  11.5 7.1 copy-start.1
  31.1 11.7 %copy-start.13 = (bf16[3,16,4096]{2,1,0:T(8,128)(2,1)S(1)}, bf16[3,16,4096]{2,1,0:T(8,128)(2,1)}, u32[]{:S(2)}) copy-start(bf16[3,16,4096]{2,1,0:T(8,128)(2,1)} %param.12) | copy-start | bytes 1179652
  31.1 11.7 %copy-start.15 = (bf16[3,4096,16]{1,2,0:T(8,128)(2,1)S(1)}, bf16[3,4096,16]{1,2,0:T(8,128)(2,1)}, u32[]{:S(2)}) copy-start(bf16[3,4096,16]{1,2,0:T(8,128)(2,1)} %param.11) | copy-start | bytes 1179652
  107.4 3.1 copy-start.2
  116.7 6.6 copy-start.14
  123.3 7.3 slice-start.1
  123.8 6.8 slice-start.2
  128.7 1.8 copy-start.11
  131.4 1.6 copy-start.5
  133.0 2.3 copy-start.23
  150.4 371.2 %all-to-all-start = ((bf16[16,1,64,4096]{3,2,1,0:T(8,128)(2,1)}), bf16[16,1,64,4096]{3,2,1,0:T(8,128)(2,1)}, u32[]{:S(2)}, u32[]{:S(2)}) async-start(bf16[16,1,64,4096]{3,2,1,0:T(8,128)(2,1)} %fusion.9), calls=%async_computation | async-start | bytes 16777216 | tf_op jit(solution)/shard_map/all_to_all | solution.py:144
  156.9 320.8 %collective-permute-start = (bf16[64,4096]{1,0:T(8,128)(2,1)}, bf16[64,4096]{1,0:T(8,128)(2,1)}, u32[]{:S(2)}, u32[]{:S(2)}) collective-permute-start(bf16[64,4096]{1,0:T(8,128)(2,1)} %get-tuple-element.73), channel_id=1, source_target_pairs={{0,1},{1,2},{2,3},{3,4},{4,5},{5,6},{6,7},{7,8},{8,9},{9,10},{10,1... | collective-permute-start | bytes 1572872 | tf_op jit(solution)/shard_map/ppermute | solution.py:25
  160.5 318.4 %collective-permute-start.1 = (bf16[64,4096]{1,0:T(8,128)(2,1)}, bf16[64,4096]{1,0:T(8,128)(2,1)}, u32[]{:S(2)}, u32[]{:S(2)}) collective-permute-start(bf16[64,4096]{1,0:T(8,128)(2,1)} %get-tuple-element.72), channel_id=1, source_target_pairs={{1,0},{2,1},{3,2},{4,3},{5,4},{6,5},{7,6},{8,7},{9,8},{10,9},{11,1... | collective-permute-start | bytes 1572872 | tf_op jit(solution)/shard_map/ppermute | solution.py:26
  174.6 265.9 %copy-start.6 = (f32[32,128,192]{1,2,0:T(8,128)S(1)}, f32[32,128,192]{1,2,0:T(8,128)}, u32[]{:S(2)}) copy-start(f32[32,128,192]{1,2,0:T(8,128)} %copy-done.5) | copy-start | bytes 9437188
  479.9 1.0 copy-start.12
  482.2 2.8 copy-start.3
  509.3 2.5 copy-start.10
  511.9 1.4 copy-start.7
  597.5 19.3 %copy-start.22 = (pred[576]{0:T(1024)(128)(4,1)S(1)}, pred[576]{0:T(1024)(128)(4,1)}, u32[]{:S(2)}) copy-start(pred[576]{0:T(1024)(128)(4,1)} %broadcast_in_dim.83) | copy-start | bytes 1732
  616.8 2.9 copy-start.16
  661.9 16.7 %copy-start.8 = (bf16[1,32,192,128]{3,2,1,0:T(8,128)(2,1)S(1)}, bf16[1,32,192,128]{3,2,1,0:T(8,128)(2,1)}, u32[]{:S(2)}) copy-start(bf16[1,32,192,128]{3,2,1,0:T(8,128)(2,1)} %slice.140) | copy-start | bytes 4718596
  661.9 16.7 %copy-start.21 = (pred[3,384]{1,0:T(4,128)(4,1)S(1)}, pred[3,384]{1,0:T(4,128)(4,1)}, u32[]{:S(2)}) copy-start(pred[3,384]{1,0:T(4,128)(4,1)} %concatenate.15) | copy-start | bytes 3460
  678.6 7.3 copy-start.20
  685.9 8.0 %copy-start.4 = (f32[32,3,64,384]{3,2,1,0:T(8,128)}, f32[32,3,64,384]{3,2,1,0:T(8,128)S(1)}, u32[]{:S(2)}) copy-start(f32[32,3,64,384]{3,2,1,0:T(8,128)S(1)} %get-tuple-element.77) | copy-start | bytes 28311556
  694.0 10.5 %copy-start.9 = (f32[32,3,64,128]{3,2,1,0:T(8,128)S(1)}, f32[32,3,64,128]{3,2,1,0:T(8,128)}, u32[]{:S(2)}) copy-start(f32[32,3,64,128]{3,2,1,0:T(8,128)} %get-tuple-element.79) | copy-start | bytes 9437188
  707.9 1.1 copy-start.17
  709.2 22.7 %slice-start = ((f32[512,128,128]{2,1,0:T(8,128)}), f32[32,128,128]{2,1,0:T(8,128)S(1)}, s32[]{:S(2)}) async-start(f32[512,128,128]{2,1,0:T(8,128)} %all-gather.5.cloned.1.call-done), calls=%async_computation.3 | async-start | bytes 4194304 | tf_op jit(solution)/shard_map/slice | solution.py:33
  709.2 22.7 %slice-start.3 = ((f32[512,128]{1,0:T(8,128)}), f32[480,128]{1,0:T(8,128)S(1)}, s32[]{:S(2)}) async-start(f32[512,128]{1,0:T(8,128)} %copy-done.18), calls=%async_computation.6 | async-start | bytes 491520 | tf_op jit(solution)/shard_map/slice | solution.py:34
  709.2 22.7 %copy-start.19 = (f32[32,128]{1,0:T(8,128)S(1)}, f32[32,128]{1,0:T(8,128)}, u32[]{:S(2)}) copy-start(f32[32,128]{1,0:T(8,128)} %slice.133) | copy-start | bytes 49156
  (1 other events, 0.7 us)
Sparse Core Ops, SparseCore 0:
  10.8 94.7 all-reduce.2
  135.4 341.5 all-gather.4
where the time goes:
time: 805 us; the launch traced here: 794 us
  blocking collectives  290 us (36%)
  local copies, waits for them, and re-layouts  183 us (23%)
  matrix products  144 us (18%)
  other arithmetic  103 us (13%)
  waiting for transfers between devices  48.9 us (6%)
  between operations  14.3 us (2%)
  starting transfers between devices  10.9 us (1%)
    all_gather x2, blocking collectives, combined_all(): pieces = jax.tree.map(lambda part: lax.all_gather(part, axis), value)  290 us
    psum x1, waiting for transfers between devices, spread(): return lax.psum(jnp.where(mine, value, jnp.zeros_like(value)), axis)  48.8 us
    dot_general x4, matrix products, apply_projection(): jnp.einsum('ptaj,pjak->ptjk', inner_rows, monarch_outer_factor, preferred...  46.8 us
    reshape x4, local copies, waits for them, and re-layouts, apply_projection(): main_part.reshape(proj_count, row_count, feature_count)  43.4 us
    add x15, other arithmetic, combine(): numer_one * factor_one[:, :, None] + numer_two * factor_two[:, :, None]  40.8 us
    dot_general x4, matrix products, apply_projection(): jnp.einsum('tai,paij->ptaj', split_rows, monarch_inner_factor, preferred_...  38 us
    dot_general x4, matrix products, apply_projection(): jnp.einsum('bcj,bjf->bcf', adapter_update, adapter_up_weight, preferred_e...  27 us
    unnamed x56, local copies, waits for them, and re-layouts  26 us
  transfers between devices with their start and end apart: 5, of which 1 were waited for; matrix products, arithmetic and copies ran while one was open for 40% of the time, Pallas kernels for 0%

commit v1 on v0

v1 whole, which is shorter than its diff:
```python
import functools

import jax
import jax.numpy as jnp
from jax import lax
from jax.experimental import pallas as pl
from jax.experimental.pallas import tpu as pltpu
from jax.sharding import PartitionSpec as P

HEADS = 32
HD = 128
BLK = 64
RAND = 3
GLOB_BLOCKS = 2
LOG2E = 1.4426950408889634


def project(tokens, inner_factor, outer_factor, down, up, groups):
    rows, width = tokens.shape
    count = inner_factor.shape[0]
    split = tokens.reshape(rows, count, count)
    inner = jnp.einsum(
        "tai,aij->taj", split, inner_factor, preferred_element_type=jnp.float32
    ).astype(jnp.bfloat16)
    low = jnp.dot(tokens, down, preferred_element_type=jnp.float32).astype(jnp.bfloat16)
    rank = low.shape[1]
    left = jnp.concatenate(
        [inner, jnp.broadcast_to(low[:, :, None], (rows, rank, count))], axis=1
    )
    lifted = jnp.transpose(up.reshape(rank, count, width // count), (1, 0, 2))
    right = jnp.concatenate([outer_factor, lifted], axis=1)
    out = jnp.einsum("taj,jak->jtk", left, right, preferred_element_type=jnp.float32)
    out = out.astype(jnp.bfloat16).reshape(groups, count // groups, rows, width // count)
    return jnp.transpose(out, (0, 2, 1, 3)).reshape(groups, rows, width // groups)


def attend_kernel(pattern_ref, q_ref, k_ref, v_ref, o_ref):
    rows = q_ref.shape[0]
    blocks = rows // BLK
    glob = GLOB_BLOCKS * BLK
    factor = float(HD) ** (-0.5) * LOG2E

    def softmax(query, keys, values, mask=None):
        scores = lax.dot_general(
            query, keys, (((1,), (1,)), ((), ())), preferred_element_type=jnp.float32
        )
        if mask is not None:
            scores = jnp.where(mask, -jnp.inf, scores)
        peak = jnp.max(scores, axis=-1, keepdims=True)
        weights = jnp.exp2((scores - peak) * factor)
        total = jnp.sum(weights, axis=-1, keepdims=True)
        mixed = jnp.dot(weights.astype(jnp.bfloat16), values, preferred_element_type=jnp.float32)
        return (mixed / total).astype(jnp.bfloat16)

    def rows_of(block):
        return pl.ds(pl.multiple_of(block * BLK, BLK), BLK)

    def one_block(block):
        picks = [block - 1, block, jnp.minimum(block + 1, blocks - 1)]
        picks += [pattern_ref[block * RAND + r] for r in range(RAND)]
        keys = jnp.concatenate([k_ref[:glob]] + [k_ref[rows_of(b)] for b in picks], axis=0)
        values = jnp.concatenate([v_ref[:glob]] + [v_ref[rows_of(b)] for b in picks], axis=0)
        place = lax.broadcasted_iota(jnp.int32, (1, keys.shape[0]), 1)
        before = (place >= glob) & (place < glob + BLK) & (block - 1 < GLOB_BLOCKS)
        after = (place >= glob + 2 * BLK) & (place < glob + 3 * BLK) & (block + 1 >= blocks)
        return softmax(q_ref[rows_of(block)], keys, values, before | after)

    o_ref[:glob] = softmax(q_ref[:glob], k_ref[...], v_ref[...])

    group = 2 if (blocks - GLOB_BLOCKS) % 2 == 0 else 1

    def body(step, carry):
        start = GLOB_BLOCKS + step * group
        outs = [one_block(start + i) for i in range(group)]
        for i in range(group):
            o_ref[rows_of(start + i)] = outs[i]
        return carry

    lax.fori_loop(0, (blocks - GLOB_BLOCKS) // group, body, 0)


def attend(pattern, query, keys, values):
    devs, rows, features = query.shape
    flat = [x.reshape(devs * rows, features) for x in (query, keys, values)]
    spec = pl.BlockSpec((devs * rows, HD), lambda h, _: (0, h))
    out = pl.pallas_call(
        attend_kernel,
        out_shape=jax.ShapeDtypeStruct(flat[0].shape, query.dtype),
        grid_spec=pltpu.PrefetchScalarGridSpec(
            num_scalar_prefetch=1,
            grid=(features // HD,),
            in_specs=[spec] * 3,
            out_specs=spec,
        ),
        compiler_params=pltpu.CompilerParams(vmem_limit_bytes=40 * 1024 * 1024),
    )(pattern, *flat)
    return out.reshape(query.shape)


def per_device(tokens, inner_factor, outer_factor, down, up, pattern):
    rows, width = tokens.shape
    devs = lax.axis_size("seq")
    swap = functools.partial(
        lax.all_to_all, axis_name="seq", split_axis=0, concat_axis=0, tiled=True
    )
    by_head = [
        swap(project(tokens, inner_factor[p], outer_factor[p], down[p], up[p], devs))
        for p in range(inner_factor.shape[0])
    ]
    mixed = attend(pattern.reshape(-1), *by_head)
    back = swap(mixed)
    return jnp.transpose(back, (1, 0, 2)).reshape(rows, width)


def solution(mesh):
    return jax.shard_map(
        per_device,
        mesh=mesh,
        in_specs=(P(("dp", "seq"), None), P(), P(), P(), P(), P("dp", None)),
        out_specs=P(("dp", "seq"), None),
        check_vma=False,
    )
```

time: 805 us -> 226 us (0.28); the launches traced: 794 us -> 226 us
  blocking collectives: 290 us -> 45 us
  local copies, waits for them, and re-layouts: 183 us -> 34.1 us
  matrix products: 144 us -> 23.1 us
  other arithmetic: 103 us -> 1.28 us
  Pallas kernels: 0 us -> 34 us
  waiting for transfers between devices: 48.9 us -> 63.1 us
  between operations: 14.3 us -> 0.16 us
  starting transfers between devices: 10.9 us -> 24.9 us
    all_gather x2 -> x0, blocking collectives: 290 us -> none  [combined_all(): pieces = jax.tree.map(lambda part: lax.all_gather(part, axis), value)]
    dot_general x18 -> x9, matrix products: 140 us -> 23.1 us  [the longest x3 10.3 us: project(): jnp.einsum('taj,jak->jtk', left, right, preferred_element_type=jnp.float32)]
    all_to_all x1 -> x3, waiting for transfers between devices: 0.01 us -> 63.1 us  [per_device(): swap(project(tokens, inner_factor[p], outer_factor[p], down[p], up[p], de...]
    add x34 -> x0, other arithmetic: 52.1 us -> none  [the longest x15 40.8 us: combine(): numer_one * factor_one[:, :, None] + numer_two * factor_two[:, :, None]]
    psum x1 -> x0, waiting for transfers between devices: 48.8 us -> none  [spread(): return lax.psum(jnp.where(mine, value, jnp.zeros_like(value)), axis)]
    all_to_all x0 -> x1, blocking collectives: none -> 45 us  [per_device(): back = swap(mixed)]
    reshape x8 -> x5, local copies, waits for them, and re-layouts: 55.5 us -> 13.1 us  [the longest x3 11.7 us: project(): jnp.transpose(out, (0, 2, 1, 3)).reshape(groups, rows, width // groups)]
    pallas_call x0 -> x1, Pallas kernels: none -> 34 us  [attend(): pl.pallas_call(attend_kernel, out_shape=jax.ShapeDtypeStruct(flat[0].shap...]
  transfers between devices with their start and end apart: 5 -> 3, of which waited for: 1 -> 3; matrix products, arithmetic and copies ran while one was open for 40% -> 14% of each run, Pallas kernels for 0% -> 0%
where the time goes in v1:
time: 226 us
  waiting for transfers between devices  63.1 us (28%)
  blocking collectives  45 us (20%)
  local copies, waits for them, and re-layouts  34.1 us (15%)
  Pallas kernels  34 us (15%)
  starting transfers between devices  24.9 us (11%)
  matrix products  23.1 us (10%)
    all_to_all x3, waiting for transfers between devices, per_device(): swap(project(tokens, inner_factor[p], outer_factor[p], down[p], up[p], de...  63.1 us
    all_to_all x1, blocking collectives, per_device(): back = swap(mixed)  45 us
    pallas_call x1, Pallas kernels, attend(): pl.pallas_call(attend_kernel, out_shape=jax.ShapeDtypeStruct(flat[0].shap...  34 us
    all_to_all x3, starting transfers between devices, per_device(): swap(project(tokens, inner_factor[p], outer_factor[p], down[p], up[p], de...  24.9 us
    unnamed x21, local copies, waits for them, and re-layouts  13.3 us
    reshape x3, local copies, waits for them, and re-layouts, project(): jnp.transpose(out, (0, 2, 1, 3)).reshape(groups, rows, width // groups)  11.7 us
    dot_general x3, matrix products, project(): jnp.einsum('taj,jak->jtk', left, right, preferred_element_type=jnp.float32)  10.3 us
    dot_general x3, matrix products, project(): jnp.einsum('tai,aij->taj', split, inner_factor, preferred_element_type=jn...  8.06 us
  transfers between devices with their start and end apart: 3, of which 3 were waited for; matrix products, arithmetic and copies ran while one was open for 14% of the time, Pallas kernels for 0%

profile of v1, /device:TPU:1, one launch (start us, length us, event | category | flops | bytes accessed | tf_op | source)
XLA Modules:
  0.0 225.6 jit_solution(12622107179608996931)
XLA Ops:
  0.0 4.0 %copy.31 = bf16[192,4096]{0,1:T(8,128)(2,1)} copy(bf16[192,4096]{1,0:T(8,128)(2,1)} %param.6) | data formatting | bytes 3145728 | tf_op args[0]
  4.0 1.4 convolution_convert_fusion.2
  5.4 3.6 %fusion.39 = (bf16[1,64,64,64]{3,2,1,0:T(8,128)(2,1)}, bf16[1,64,64,64]{3,2,1,0:T(8,128)(2,1)}, bf16[1,64,64,64]{3,2,1,0:T(8,128)(2,1)}) fusion(bf16[3,64,64,64]{3,2,1,0:T(8,128)(2,1)} %param.8), kind=kLoop, calls=%fused_computation.42 | loop fusion | bytes 3145728 | tf_op jit(solution)/shard_map/slice | solution.py:107
  9.0 1.7 copy.47
  10.7 1.3 copy.33
  12.0 2.7 %convert_bitcast_fusion.2 = bf16[192,64,64]{0,2,1:T(8,128)(2,1)S(1)} fusion(bf16[192,64,64]{0,2,1:T(8,128)(2,1)} %bitcast.71, bf16[3,64,64,64]{3,2,1,0:T(8,128)(2,1)} %param.7), kind=kOutput, calls=%fused_computation.11 | convolution fusion | flops 101449728 | bytes 4718592 | tf_op jit(solution)/shard_map/tai,aij->taj/dot_general | solution.py:22
  15.2 0.8 copy-done.5
  16.0 3.5 %fusion.6 = bf16[64,192,64]{1,2,0:T(8,128)(2,1)} fusion(bf16[192,80,64]{0,2,1:T(8,128)(2,1)S(1)} %pad_maximum_fusion, bf16[64,16,64]{1,2,0:T(8,128)(2,1)S(1)} %bitcast.83, bf16[64,64,64]{1,2,0:T(8,128)(2,1)S(1)} %bitcast.78), kind=kOutput, calls=%fused_computation.12 | convolution fusion | flops 127926272 | bytes 4194304 | tf_op jit(solution)/shard_map/taj,jak->jtk/dot_general | solution.py:32
  19.4 3.9 %copy.35 = bf16[16,192,256]{2,1,0:T(8,128)(2,1)} copy(bf16[16,192,256]{1,2,0:T(8,128)(2,1)} %bitcast.74) | data formatting | bytes 3145728 | tf_op jit(solution)/shard_map/reshape | solution.py:34
  23.3 7.3 %all-to-all-start = ((bf16[16,192,256]{2,1,0:T(8,128)(2,1)}), bf16[16,192,256]{2,1,0:T(8,128)(2,1)S(1)}, u32[]{:S(2)}, u32[]{:S(2)}) async-start(bf16[16,192,256]{2,1,0:T(8,128)(2,1)} %copy.35), calls=%async_computation | async-start | bytes 3145728 | tf_op jit(solution)/shard_map/all_to_all | solution.py:107
  30.7 2.3 %copy.49 = bf16[1,64,64,64]{2,3,1,0:T(8,128)(2,1)} copy(bf16[1,64,64,64]{3,2,1,0:T(8,128)(2,1)} %get-tuple-element.6) | data formatting | bytes 1048576
  32.9 1.3 copy.38
  34.3 1.4 convolution_convert_fusion.1
  35.7 2.7 %convert_bitcast_fusion.1 = bf16[192,64,64]{0,2,1:T(8,128)(2,1)S(1)} fusion(bf16[192,64,64]{0,2,1:T(8,128)(2,1)} %bitcast.72, bf16[3,64,64,64]{3,2,1,0:T(8,128)(2,1)} %param.7), kind=kOutput, calls=%fused_computation.10 | convolution fusion | flops 101449728 | bytes 4718592 | tf_op jit(solution)/shard_map/tai,aij->taj/dot_general | solution.py:22
  38.9 0.8 copy-done.2
  40.0 3.4 %fusion.9 = bf16[64,192,64]{1,2,0:T(8,128)(2,1)} fusion(bf16[192,80,64]{0,2,1:T(8,128)(2,1)S(1)} %pad_maximum_fusion.1, bf16[64,16,64]{1,2,0:T(8,128)(2,1)S(1)} %bitcast.82, bf16[64,64,64]{1,2,0:T(8,128)(2,1)S(1)} %bitcast.80), kind=kOutput, calls=%fused_computation.13 | convolution fusion | flops 127926272 | bytes 4194304 | tf_op jit(solution)/shard_map/taj,jak->jtk/dot_general | solution.py:32
  43.4 3.9 %copy.40 = bf16[16,192,256]{2,1,0:T(8,128)(2,1)} copy(bf16[16,192,256]{1,2,0:T(8,128)(2,1)} %bitcast.75) | data formatting | bytes 3145728 | tf_op jit(solution)/shard_map/reshape | solution.py:34
  47.3 15.7 %all-to-all-done = bf16[16,192,256]{2,1,0:T(8,128)(2,1)S(1)} async-done(((bf16[16,192,256]{2,1,0:T(8,128)(2,1)}), bf16[16,192,256]{2,1,0:T(8,128)(2,1)S(1)}, u32[]{:S(2)}, u32[]{:S(2)}) %all-to-all-start) | async-done | bytes 1572896 | tf_op jit(solution)/shard_map/all_to_all | solution.py:107
  63.0 8.8 %all-to-all-start.1 = ((bf16[16,192,256]{2,1,0:T(8,128)(2,1)}), bf16[16,192,256]{2,1,0:T(8,128)(2,1)S(1)}, u32[]{:S(2)}, u32[]{:S(2)}) async-start(bf16[16,192,256]{2,1,0:T(8,128)(2,1)} %copy.40), calls=%async_computation.1 | async-start | bytes 3145728 | tf_op jit(solution)/shard_map/all_to_all | solution.py:107
  71.8 2.3 %copy.51 = bf16[1,64,64,64]{2,3,1,0:T(8,128)(2,1)} copy(bf16[1,64,64,64]{3,2,1,0:T(8,128)(2,1)} %get-tuple-element.5) | data formatting | bytes 1048576
  74.0 1.3 copy.43
  75.4 1.9 convolution_convert_fusion
  77.3 2.7 %convert_bitcast_fusion = bf16[192,64,64]{0,2,1:T(8,128)(2,1)S(1)} fusion(bf16[192,64,64]{0,2,1:T(8,128)(2,1)} %bitcast.73, bf16[3,64,64,64]{3,2,1,0:T(8,128)(2,1)} %param.7), kind=kOutput, calls=%fused_computation.9 | convolution fusion | flops 101449728 | bytes 4718592 | tf_op jit(solution)/shard_map/tai,aij->taj/dot_general | solution.py:22
  80.5 0.8 copy-done.1
  81.6 3.4 %fusion.12 = bf16[64,192,64]{1,2,0:T(8,128)(2,1)} fusion(bf16[192,80,64]{0,2,1:T(8,128)(2,1)S(1)} %pad_maximum_fusion.2, bf16[64,16,64]{1,2,0:T(8,128)(2,1)S(1)} %bitcast.81, bf16[64,64,64]{1,2,0:T(8,128)(2,1)S(1)} %bitcast.79), kind=kOutput, calls=%fused_computation.14 | convolution fusion | flops 127926272 | bytes 4194304 | tf_op jit(solution)/shard_map/taj,jak->jtk/dot_general | solution.py:32
  85.0 3.9 %copy.45 = bf16[16,192,256]{2,1,0:T(8,128)(2,1)} copy(bf16[16,192,256]{1,2,0:T(8,128)(2,1)} %bitcast.76) | data formatting | bytes 3145728 | tf_op jit(solution)/shard_map/reshape | solution.py:34
  88.9 15.2 %all-to-all-done.1 = bf16[16,192,256]{2,1,0:T(8,128)(2,1)S(1)} async-done(((bf16[16,192,256]{2,1,0:T(8,128)(2,1)}), bf16[16,192,256]{2,1,0:T(8,128)(2,1)S(1)}, u32[]{:S(2)}, u32[]{:S(2)}) %all-to-all-start.1) | async-done | bytes 1572896 | tf_op jit(solution)/shard_map/all_to_all | solution.py:107
  104.1 8.8 %all-to-all-start.2 = ((bf16[16,192,256]{2,1,0:T(8,128)(2,1)}), bf16[16,192,256]{2,1,0:T(8,128)(2,1)}, u32[]{:S(2)}, u32[]{:S(2)}) async-start(bf16[16,192,256]{2,1,0:T(8,128)(2,1)} %copy.45), calls=%async_computation.2 | async-start | bytes 3145728 | tf_op jit(solution)/shard_map/all_to_all | solution.py:107
  113.1 32.2 %all-to-all-done.2 = bf16[16,192,256]{2,1,0:T(8,128)(2,1)} async-done(((bf16[16,192,256]{2,1,0:T(8,128)(2,1)}), bf16[16,192,256]{2,1,0:T(8,128)(2,1)}, u32[]{:S(2)}, u32[]{:S(2)}) %all-to-all-start.2) | async-done | bytes 1572896 | tf_op jit(solution)/shard_map/all_to_all | solution.py:107
  145.3 34.0 %shard_map.64 = bf16[3072,256]{1,0:T(8,128)(2,1)S(1)} custom-call(s32[144]{0:T(256)S(1)} %reshape.44.pattern_ref, bf16[3072,256]{1,0:T(8,128)(2,1)S(1)} %bitcast.68, bf16[3072,256]{1,0:T(8,128)(2,1)S(1)} %bitcast.69, bf16[3072,256]{1,0:T(8,128)(2,1)} %bitcast.30.v_ref), custom_call_target="tpu_custom_call" | custom-call | tf_op jit(solution)/shard_map/pallas_call | solution.py:86
  179.3 45.0 %all_to_all.20 = bf16[16,192,256]{2,1,0:T(8,128)(2,1)S(1)} all-to-all(bf16[16,192,256]{2,1,0:T(8,128)(2,1)S(1)} %bitcast.70), channel_id=1, replica_groups=mesh['dp'=2,'seq'=16] {'seq'}, dimensions={0} | all-to-all | bytes 3145728 | tf_op jit(solution)/shard_map/all_to_all | solution.py:111
  224.3 1.3 copy.53
  (22 shorter events, 2.3 us)
Async XLA Ops:
  0.0 4.0 %copy-start = (bf16[192,4096]{1,0:T(8,128)(2,1)S(1)}, bf16[192,4096]{1,0:T(8,128)(2,1)}, u32[]{:S(2)}) copy-start(bf16[192,4096]{1,0:T(8,128)(2,1)} %param.6) | copy-start | bytes 4718596
  9.0 1.7 copy-start.6
  14.7 1.2 copy-start.5
  23.3 39.7 %all-to-all-start = ((bf16[16,192,256]{2,1,0:T(8,128)(2,1)}), bf16[16,192,256]{2,1,0:T(8,128)(2,1)S(1)}, u32[]{:S(2)}, u32[]{:S(2)}) async-start(bf16[16,192,256]{2,1,0:T(8,128)(2,1)} %copy.35), calls=%async_computation | async-start | bytes 3145728 | tf_op jit(solution)/shard_map/all_to_all | solution.py:107
  38.4 1.2 copy-start.2
  38.5 1.5 copy-start.4
  63.0 41.1 %all-to-all-start.1 = ((bf16[16,192,256]{2,1,0:T(8,128)(2,1)}), bf16[16,192,256]{2,1,0:T(8,128)(2,1)S(1)}, u32[]{:S(2)}, u32[]{:S(2)}) async-start(bf16[16,192,256]{2,1,0:T(8,128)(2,1)} %copy.40), calls=%async_computation.1 | async-start | bytes 3145728 | tf_op jit(solution)/shard_map/all_to_all | solution.py:107
  80.0 1.2 copy-start.1
  80.0 1.5 copy-start.3
  88.9 24.0 %copy-start.7 = (s32[48,3]{0,1:T(4,128)S(1)}, s32[48,3]{0,1:T(4,128)}, u32[]{:S(2)}) copy-start(s32[48,3]{0,1:T(4,128)} %param.11) | copy-start | bytes 1732
  104.1 41.2 %all-to-all-start.2 = ((bf16[16,192,256]{2,1,0:T(8,128)(2,1)}), bf16[16,192,256]{2,1,0:T(8,128)(2,1)}, u32[]{:S(2)}, u32[]{:S(2)}) async-start(bf16[16,192,256]{2,1,0:T(8,128)(2,1)} %copy.45), calls=%async_computation.2 | async-start | bytes 3145728 | tf_op jit(solution)/shard_map/all_to_all | solution.py:107

commit v2 on v1

--- a/solution.py
+++ b/solution.py
@@ -30,8 +30,13 @@
     lifted = jnp.transpose(up.reshape(rank, count, width // count), (1, 0, 2))
     right = jnp.concatenate([outer_factor, lifted], axis=1)
     out = jnp.einsum("taj,jak->jtk", left, right, preferred_element_type=jnp.float32)
-    out = out.astype(jnp.bfloat16).reshape(groups, count // groups, rows, width // count)
-    return jnp.transpose(out, (0, 2, 1, 3)).reshape(groups, rows, width // groups)
+    heads = HEADS // groups
+    out = out.astype(jnp.bfloat16)
+    out = out.reshape(groups, heads, count // HEADS, rows, width // count)
+    return [
+        jnp.transpose(out[:, h], (0, 2, 1, 3)).reshape(groups, rows, width // HEADS)
+        for h in range(heads)
+    ]
 
 
 def attend_kernel(pattern_ref, q_ref, k_ref, v_ref, o_ref):
@@ -79,37 +84,64 @@
     lax.fori_loop(0, (blocks - GLOB_BLOCKS) // group, body, 0)
 
 
-def attend(pattern, query, keys, values):
-    devs, rows, features = query.shape
-    flat = [x.reshape(devs * rows, features) for x in (query, keys, values)]
-    spec = pl.BlockSpec((devs * rows, HD), lambda h, _: (0, h))
+def attend(pattern, head, keys, value_query):
+    devs, rows, features = keys.shape
+    tokens = devs * rows
+    keys = keys.reshape(tokens, features)
+    value_query = value_query.reshape(tokens, 2 * HD)
+    glob = GLOB_BLOCKS * BLK
+    pairs = tokens * (glob + (3 + RAND) * BLK) + glob * tokens
+
+    def column(place):
+        return pl.BlockSpec((tokens, HD), lambda _, __: (0, place))
+
     out = pl.pallas_call(
         attend_kernel,
-        out_shape=jax.ShapeDtypeStruct(flat[0].shape, query.dtype),
+        out_shape=jax.ShapeDtypeStruct((tokens, HD), keys.dtype),
         grid_spec=pltpu.PrefetchScalarGridSpec(
             num_scalar_prefetch=1,
-            grid=(features // HD,),
-            in_specs=[spec] * 3,
-            out_specs=spec,
+            grid=(1,),
+            in_specs=[column(1), column(head), column(0)],
+            out_specs=column(0),
         ),
         compiler_params=pltpu.CompilerParams(vmem_limit_bytes=40 * 1024 * 1024),
-    )(pattern, *flat)
-    return out.reshape(query.shape)
+        cost_estimate=pl.CostEstimate(
+            flops=8 * pairs * HD, bytes_accessed=8 * tokens * HD, transcendentals=pairs
+        ),
+    )(pattern, value_query, keys, value_query)
+    return out.reshape(devs, rows, HD)
 
 
 def per_device(tokens, inner_factor, outer_factor, down, up, pattern):
     rows, width = tokens.shape
     devs = lax.axis_size("seq")
+    heads = HEADS // devs
     swap = functools.partial(
         lax.all_to_all, axis_name="seq", split_axis=0, concat_axis=0, tiled=True
     )
-    by_head = [
-        swap(project(tokens, inner_factor[p], outer_factor[p], down[p], up[p], devs))
-        for p in range(inner_factor.shape[0])
-    ]
-    mixed = attend(pattern.reshape(-1), *by_head)
-    back = swap(mixed)
-    return jnp.transpose(back, (1, 0, 2)).reshape(rows, width)
+    query, keys, values = (
+        functools.partial(
+            project, tokens, inner_factor[p], outer_factor[p], down[p], up[p], devs
+        )
+        for p in range(3)
+    )
+    keys = swap(jnp.concatenate(keys(), axis=2))
+    pairs = [jnp.concatenate(both, axis=2) for both in zip(values(), query())]
+    named = pattern.reshape(-1)
+    arrived = keys
+    mixed, back = None, []
+    for h in range(heads):
+        pair, arrived = lax.optimization_barrier((pairs[h], arrived))
+        pair = swap(pair)
+        if h:
+            pair, mixed = lax.optimization_barrier((pair, mixed))
+            back.append(swap(mixed))
+        mixed = attend(named, h, keys, pair)
+        if h:
+            mixed, back[-1] = lax.optimization_barrier((mixed, back[-1]))
+        arrived = pair
+    back.append(swap(mixed))
+    return jnp.transpose(jnp.stack(back), (2, 1, 0, 3)).reshape(rows, width)
 
 
 def solution(mesh):

time: 226 us -> 212 us (0.938)
  blocking collectives: 45 us -> 26.1 us
  waiting for transfers between devices: 63.1 us -> 50.8 us
  starting transfers between devices: 24.9 us -> 33.7 us
  other arithmetic: 1.28 us -> 8.11 us
  local copies, waits for them, and re-layouts: 34.1 us -> 39.7 us
  matrix products: 23.1 us -> 18.3 us
    all_to_all x1, blocking collectives: 45 us -> 26.1 us  [per_device(): back.append(swap(mixed))]
    all_to_all x3 -> x4, waiting for transfers between devices: 63.1 us -> 50.8 us  [the longest x2 43.8 us: per_device(): pair = swap(pair)]
    reshape x5 -> x2, local copies, waits for them, and re-layouts: 13.1 us -> 2.51 us  [the longest x1 2.39 us: per_device(): return jnp.transpose(jnp.stack(back), (2, 1, 0, 3)).reshape(rows, width)]
    all_to_all x3 -> x4, starting transfers between devices: 24.9 us -> 33.7 us  [the longest x2 17.6 us: per_device(): pair = swap(pair)]
    optimization_barrier x0 -> x2, local copies, waits for them, and re-layouts: none -> 7.76 us  [per_device(): pair, arrived = lax.optimization_barrier((pairs[h], arrived))]
    concatenate x0 -> x3, other arithmetic: none -> 6.68 us  [the longest x2 4.99 us: per_device(): pairs = [jnp.concatenate(both, axis=2) for both in zip(values(), query())]]
    concatenate x0 -> x1, local copies, waits for them, and re-layouts: none -> 3.88 us  [per_device(): keys = swap(jnp.concatenate(keys(), axis=2))]
    dot_general x3, matrix products: 10.3 us -> 6.47 us  [project(): jnp.einsum('taj,jak->jtk', left, right, preferred_element_type=jnp.float32)]
  transfers between devices with their start and end apart: 3 -> 4, of which waited for: 3 -> 4; matrix products, arithmetic and copies ran while one was open for 14% -> 13% of each run, Pallas kernels for 0% -> 16%
where the time goes in v2:
time: 212 us; the launch traced here: 211 us
  waiting for transfers between devices  50.8 us (24%)
  local copies, waits for them, and re-layouts  39.7 us (19%)
  Pallas kernels  34.4 us (16%)
  starting transfers between devices  33.7 us (16%)
  blocking collectives  26.1 us (12%)
  matrix products  18.3 us (9%)
  other arithmetic  8.11 us (4%)
    all_to_all x2, waiting for transfers between devices, per_device(): pair = swap(pair)  43.8 us
    pallas_call x2, Pallas kernels, attend(): pl.pallas_call(attend_kernel, out_shape=jax.ShapeDtypeStruct((tokens, HD)...  34.4 us
    all_to_all x1, blocking collectives, per_device(): back.append(swap(mixed))  26.1 us
    all_to_all x2, starting transfers between devices, per_device(): pair = swap(pair)  17.6 us
    unnamed x25, local copies, waits for them, and re-layouts  13.8 us
    all_to_all x1, starting transfers between devices, per_device(): back.append(swap(mixed))  8.76 us
    optimization_barrier x2, local copies, waits for them, and re-layouts, per_device(): pair, arrived = lax.optimization_barrier((pairs[h], arrived))  7.76 us
    dot_general x3, matrix products, project(): jnp.einsum('tai,aij->taj', split, inner_factor, preferred_element_type=jn...  7.37 us
  transfers between devices with their start and end apart: 4, of which 4 were waited for; matrix products, arithmetic and copies ran while one was open for 13% of the time, Pallas kernels for 16%

profile of v2, /device:TPU:1, one launch (start us, length us, event | category | flops | bytes accessed | tf_op | source)
XLA Modules:
  0.0 211.3 jit_solution(5471598845585562195)
XLA Ops:
  0.0 4.0 %copy.40 = bf16[192,4096]{0,1:T(8,128)(2,1)} copy(bf16[192,4096]{1,0:T(8,128)(2,1)} %param.6) | data formatting | bytes 3145728 | tf_op args[0]
  4.0 1.4 convolution_convert_fusion
  5.4 3.6 %fusion.39 = (bf16[1,64,64,64]{3,2,1,0:T(8,128)(2,1)}, bf16[1,64,64,64]{3,2,1,0:T(8,128)(2,1)}, bf16[1,64,64,64]{3,2,1,0:T(8,128)(2,1)}) fusion(bf16[3,64,64,64]{3,2,1,0:T(8,128)(2,1)} %param.8), kind=kLoop, calls=%fused_computation.46 | loop fusion | bytes 3145728 | tf_op jit(solution)/shard_map/slice | solution.py:124
  9.0 1.7 copy.70
  12.0 2.7 %convert_bitcast_fusion = bf16[192,64,64]{0,2,1:T(8,128)(2,1)S(1)} fusion(bf16[192,64,64]{0,2,1:T(8,128)(2,1)} %bitcast.106, bf16[3,64,64,64]{3,2,1,0:T(8,128)(2,1)} %param.7), kind=kOutput, calls=%fused_computation.12 | convolution fusion | flops 101449728 | bytes 4718592 | tf_op jit(solution)/shard_map/tai,aij->taj/dot_general | solution.py:22
  16.0 2.1 %fusion.12 = bf16[64,192,64]{1,2,0:T(8,128)(2,1)S(1)} fusion(bf16[192,80,64]{0,2,1:T(8,128)(2,1)S(1)} %pad_maximum_fusion.2, bf16[64,16,64]{1,2,0:T(8,128)(2,1)S(1)} %bitcast.117, bf16[64,64,64]{1,2,0:T(8,128)(2,1)S(1)} %bitcast.116), kind=kOutput, calls=%fused_computation.17 | convolution fusion | flops 127926272 | bytes 4194304 | tf_op jit(solution)/shard_map/taj,jak->jtk/dot_general | solution.py:32
  18.3 1.7 pad_maximum_fusion.5
  20.0 3.9 %copy.58 = bf16[16,192,256]{2,1,0:T(8,128)(2,1)} copy(bf16[16,192,256]{1,2,0:T(8,128)(2,1)} %pad_maximum_fusion.5) | data formatting | bytes 3145728 | tf_op jit(solution)/shard_map/concatenate | solution.py:128
  23.9 7.3 %all-to-all-start = ((bf16[16,192,256]{2,1,0:T(8,128)(2,1)}), bf16[16,192,256]{2,1,0:T(8,128)(2,1)S(1)}, u32[]{:S(2)}, u32[]{:S(2)}) async-start(bf16[16,192,256]{2,1,0:T(8,128)(2,1)} %copy.58), calls=%async_computation | async-start | bytes 3145728 | tf_op jit(solution)/shard_map/all_to_all | solution.py:128
  31.2 2.3 %copy.62 = bf16[1,64,64,64]{2,3,1,0:T(8,128)(2,1)} copy(bf16[1,64,64,64]{3,2,1,0:T(8,128)(2,1)} %get-tuple-element.19) | data formatting | bytes 1048576
  34.8 2.3 %copy.65 = bf16[1,64,64,64]{2,3,1,0:T(8,128)(2,1)} copy(bf16[1,64,64,64]{3,2,1,0:T(8,128)(2,1)} %get-tuple-element.18) | data formatting | bytes 1048576
  38.4 1.4 convolution_convert_fusion.2
  39.8 2.7 %convert_bitcast_fusion.2 = bf16[192,64,64]{0,2,1:T(8,128)(2,1)S(1)} fusion(bf16[192,64,64]{0,2,1:T(8,128)(2,1)} %bitcast.107, bf16[3,64,64,64]{3,2,1,0:T(8,128)(2,1)} %param.7), kind=kOutput, calls=%fused_computation.14 | convolution fusion | flops 101449728 | bytes 4718592 | tf_op jit(solution)/shard_map/tai,aij->taj/dot_general | solution.py:22
  43.0 1.6 convolution_convert_fusion.1
  44.6 2.0 convert_bitcast_fusion.1
  48.2 2.1 %fusion.6 = bf16[64,192,64]{1,2,0:T(8,128)(2,1)S(1)} fusion(bf16[192,80,64]{0,2,1:T(8,128)(2,1)S(1)} %pad_maximum_fusion, bf16[64,16,64]{1,2,0:T(8,128)(2,1)S(1)} %bitcast.115, bf16[64,64,64]{1,2,0:T(8,128)(2,1)S(1)} %bitcast.114), kind=kOutput, calls=%fused_computation.15 | convolution fusion | flops 127926272 | bytes 4194304 | tf_op jit(solution)/shard_map/taj,jak->jtk/dot_general | solution.py:32
  52.3 2.2 %fusion.9 = bf16[64,192,64]{1,2,0:T(8,128)(2,1)S(1)} fusion(bf16[192,80,64]{0,2,1:T(8,128)(2,1)S(1)} %pad_maximum_fusion.1, bf16[64,16,64]{1,2,0:T(8,128)(2,1)S(1)} %bitcast.113, bf16[64,64,64]{1,2,0:T(8,128)(2,1)S(1)} %bitcast.112), kind=kOutput, calls=%fused_computation.16 | convolution fusion | flops 127926272 | bytes 4194304 | tf_op jit(solution)/shard_map/taj,jak->jtk/dot_general | solution.py:32
  55.6 1.7 pad_maximum_fusion.4
  57.3 6.2 %all-to-all-done = bf16[16,192,256]{2,1,0:T(8,128)(2,1)S(1)} async-done(((bf16[16,192,256]{2,1,0:T(8,128)(2,1)}), bf16[16,192,256]{2,1,0:T(8,128)(2,1)S(1)}, u32[]{:S(2)}, u32[]{:S(2)}) %all-to-all-start) | async-done | bytes 1572896 | tf_op jit(solution)/shard_map/all_to_all | solution.py:128
  63.5 3.9 %copy.59 = bf16[16,192,256]{2,1,0:T(8,128)(2,1)} copy(bf16[16,192,256]{1,2,0:T(8,128)(2,1)} %pad_maximum_fusion.4) | data formatting | bytes 3145728 | tf_op jit(solution)/shard_map/optimization_barrier | solution.py:134
  67.4 8.8 %all-to-all-start.1 = ((bf16[16,192,256]{2,1,0:T(8,128)(2,1)}), bf16[16,192,256]{2,1,0:T(8,128)(2,1)S(1)}, u32[]{:S(2)}, u32[]{:S(2)}) async-start(bf16[16,192,256]{2,1,0:T(8,128)(2,1)} %copy.59), calls=%async_computation.1 | async-start | bytes 3145728 | tf_op jit(solution)/shard_map/all_to_all | solution.py:135
  76.2 3.3 %pad_maximum_fusion.3 = bf16[16,192,256]{1,2,0:T(8,128)(2,1)} fusion(bf16[16,192,128]{1,2,0:T(8,128)(2,1)} %bitcast.119, bf16[16,192,128]{1,2,0:T(8,128)(2,1)} %bitcast.118), kind=kLoop, calls=%fused_computation.9 | loop fusion | flops 3145728 | bytes 3145728 | tf_op jit(solution)/shard_map/concatenate | solution.py:129
  79.5 29.1 %all-to-all-done.1 = bf16[16,192,256]{2,1,0:T(8,128)(2,1)S(1)} async-done(((bf16[16,192,256]{2,1,0:T(8,128)(2,1)}), bf16[16,192,256]{2,1,0:T(8,128)(2,1)S(1)}, u32[]{:S(2)}, u32[]{:S(2)}) %all-to-all-start.1) | async-done | bytes 1572896 | tf_op jit(solution)/shard_map/all_to_all | solution.py:135
  108.5 3.9 %copy.60 = bf16[16,192,256]{2,1,0:T(8,128)(2,1)} copy(bf16[16,192,256]{1,2,0:T(8,128)(2,1)} %pad_maximum_fusion.3) | data formatting | bytes 3145728 | tf_op jit(solution)/shard_map/optimization_barrier | solution.py:134
  112.4 8.9 %all-to-all-start.2 = ((bf16[16,192,256]{2,1,0:T(8,128)(2,1)}), bf16[16,192,256]{2,1,0:T(8,128)(2,1)}, u32[]{:S(2)}, u32[]{:S(2)}) async-start(bf16[16,192,256]{2,1,0:T(8,128)(2,1)} %copy.60), calls=%async_computation.2 | async-start | bytes 3145728 | tf_op jit(solution)/shard_map/all_to_all | solution.py:135
  121.5 16.6 %shard_map.64 = bf16[3072,128]{1,0:T(8,128)(2,1)S(1)} custom-call(s32[144]{0:T(256)S(1)} %reshape.57.pattern_ref, bf16[3072,256]{1,0:T(8,128)(2,1)S(1)} %bitcast.102, bf16[3072,256]{1,0:T(8,128)(2,1)S(1)} %bitcast.100, bf16[3072,256]{1,0:T(8,128)(2,1)S(1)} %bitcast.103), custom_call_target="tpu_custom_call" | custom-call | flops 2013265920 | bytes 3145728 | tf_op jit(solution)/shard_map/pallas_call | solution.py:98
  139.0 14.7 %all-to-all-done.2 = bf16[16,192,256]{2,1,0:T(8,128)(2,1)} async-done(((bf16[16,192,256]{2,1,0:T(8,128)(2,1)}), bf16[16,192,256]{2,1,0:T(8,128)(2,1)}, u32[]{:S(2)}, u32[]{:S(2)}) %all-to-all-start.2) | async-done | bytes 1572896 | tf_op jit(solution)/shard_map/all_to_all | solution.py:135
  153.7 8.8 %all-to-all-start.3 = ((bf16[16,192,128]{2,1,0:T(8,128)(2,1)}), bf16[16,192,128]{2,1,0:T(8,128)(2,1)S(1)}, u32[]{:S(2)}, u32[]{:S(2)}) async-start(bf16[16,192,128]{2,1,0:T(8,128)(2,1)} %bitcast.104), calls=%async_computation.3 | async-start | bytes 1572864 | tf_op jit(solution)/shard_map/all_to_all | solution.py:138
  162.5 17.8 %shard_map.65 = bf16[3072,128]{1,0:T(8,128)(2,1)S(1)} custom-call(s32[144]{0:T(256)S(1)} %reshape.57.pattern_ref, bf16[3072,256]{1,0:T(8,128)(2,1)} %bitcast.43.q_ref.v_ref, bf16[3072,256]{1,0:T(8,128)(2,1)S(1)} %bitcast.101, bf16[3072,256]{1,0:T(8,128)(2,1)} %bitcast.43.q_ref.v_ref), custom_call_target="tpu_custom_call" | custom-call | flops 2013265920 | bytes 3145728 | tf_op jit(solution)/shard_map/pallas_call | solution.py:98
  181.0 26.1 %all_to_all.25 = bf16[16,192,128]{2,1,0:T(8,128)(2,1)S(1)} all-to-all(bf16[16,192,128]{2,1,0:T(8,128)(2,1)S(1)} %bitcast.105), channel_id=1, replica_groups=mesh['dp'=2,'seq'=16] {'seq'}, dimensions={0} | all-to-all | bytes 1572864 | tf_op jit(solution)/shard_map/all_to_all | solution.py:143
  207.2 1.6 copy.61
  208.9 2.4 %reshape.73 = bf16[192,4096]{1,0:T(8,128)(2,1)} reshape(bf16[192,16,2,128]{3,2,1,0:T(2,128)(2,1)S(1)} %copy.61) | data formatting | bytes 3145728 | tf_op jit(solution)/shard_map/reshape | solution.py:144
  (37 shorter events, 12.5 us)
Async XLA Ops:
  0.0 4.0 %copy-start.2 = (bf16[192,4096]{1,0:T(8,128)(2,1)S(1)}, bf16[192,4096]{1,0:T(8,128)(2,1)}, u32[]{:S(2)}) copy-start(bf16[192,4096]{1,0:T(8,128)(2,1)} %param.6) | copy-start | bytes 4718596
  9.0 1.7 copy-start.8
  14.8 1.2 copy-start.7
  23.9 39.7 %all-to-all-start = ((bf16[16,192,256]{2,1,0:T(8,128)(2,1)}), bf16[16,192,256]{2,1,0:T(8,128)(2,1)S(1)}, u32[]{:S(2)}, u32[]{:S(2)}) async-start(bf16[16,192,256]{2,1,0:T(8,128)(2,1)} %copy.58), calls=%async_computation | async-start | bytes 3145728 | tf_op jit(solution)/shard_map/all_to_all | solution.py:128
  42.6 2.0 copy-start.1
  46.7 1.2 copy-start.5
  46.7 1.5 copy-start.6
  50.4 1.4 copy-start.3
  50.4 1.9 copy-start.4
  67.4 41.1 %all-to-all-start.1 = ((bf16[16,192,256]{2,1,0:T(8,128)(2,1)}), bf16[16,192,256]{2,1,0:T(8,128)(2,1)S(1)}, u32[]{:S(2)}, u32[]{:S(2)}) async-start(bf16[16,192,256]{2,1,0:T(8,128)(2,1)} %copy.59), calls=%async_computation.1 | async-start | bytes 3145728 | tf_op jit(solution)/shard_map/all_to_all | solution.py:135
  112.4 8.9 %copy-start.9 = (s32[48,3]{0,1:T(4,128)S(1)}, s32[48,3]{0,1:T(4,128)}, u32[]{:S(2)}) copy-start(s32[48,3]{0,1:T(4,128)} %param.11) | copy-start | bytes 1732
  112.4 41.3 %all-to-all-start.2 = ((bf16[16,192,256]{2,1,0:T(8,128)(2,1)}), bf16[16,192,256]{2,1,0:T(8,128)(2,1)}, u32[]{:S(2)}, u32[]{:S(2)}) async-start(bf16[16,192,256]{2,1,0:T(8,128)(2,1)} %copy.60), calls=%async_computation.2 | async-start | bytes 3145728 | tf_op jit(solution)/shard_map/all_to_all | solution.py:135
  138.1 0.9 copy-start
  153.7 27.3 %all-to-all-start.3 = ((bf16[16,192,128]{2,1,0:T(8,128)(2,1)}), bf16[16,192,128]{2,1,0:T(8,128)(2,1)S(1)}, u32[]{:S(2)}, u32[]{:S(2)}) async-start(bf16[16,192,128]{2,1,0:T(8,128)(2,1)} %bitcast.104), calls=%async_computation.3 | async-start | bytes 1572864 | tf_op jit(solution)/shard_map/all_to_all | solution.py:138
